TPU v7x, 512 devices: a whole 4x4x16 slice. The times are simulated.
512 devices in a mesh: gx: 32 (over x, z_lo, core), gy: 16 (over y, z_hi).
Axes of the slice: x: 4, y: 4, z: 16 (z_hi: 4, z_lo: 4; z = z_hi * 4 + z_lo), core: 2. Of those that a mesh axis runs over, the one named last changes fastest.
Arguments:
- state_field: float32 [128, 128, 2304], P('gx', 'gy'), may hold values from -6 to 6
- conv_first: float32 [3, 3, 36, 108], replicated, may hold values from -0.1875 to 0.1875
- conv_second: float32 [3, 3, 36, 108], replicated, may hold values from -0.1875 to 0.1875
- spec_real: float32 [32, 32, 36, 432], P('gx', 'gy'), may hold values from -12 to 12
- spec_imag: float32 [32, 32, 36, 432], P('gx', 'gy'), may hold values from -12 to 12
Outputs:
- layer_out: float32 [128, 128, 2304], P('gx', 'gy')
All inputs are finite; a program needn't handle non-finite values.
Results may differ from a plain program's by a relative error of at most 0.00007.
Values sent between devices are 32-bit elements; how exact they have to be, the bound alone decides.
A program may use at most 128 MiB of HBM per device.

v0:
```python
import jax
import jax.numpy as jnp
from jax import lax
from jax.sharding import PartitionSpec as P

C = 36
Z = 64
MX = 16
MY = 16
MZ = 12


highest = lax.Precision.HIGHEST
two_pi = 6.283185307179586


def with_halo(cells, sides, width):
    for axis, dim in sides:
        count = lax.axis_size(axis)
        ends = count - 1
        head = lax.slice_in_dim(cells, 0, width, axis=dim)
        tail = lax.slice_in_dim(cells, cells.shape[dim] - width, cells.shape[dim], axis=dim)
        cells = jnp.concatenate(
            [
                lax.ppermute(tail, axis, [(i, (i + 1) % count) for i in range(ends)]),
                cells,
                lax.ppermute(head, axis, [((i + 1) % count, i) for i in range(ends)]),
            ],
            axis=dim,
        )
    return cells


def matmul(left, right):
    return jnp.dot(left, right, precision=highest)


def kept_modes(mode_count, length):
    places = jnp.arange(2 * mode_count, dtype=jnp.int32)
    return jnp.where(places < mode_count, places, places + length - 2 * mode_count)


def angle_table(first_index, second_index, length):
    product = first_index[:, None] * second_index[None, :] % length
    angles = product.astype(jnp.float32) * (two_pi / length)
    return (jnp.cos(angles), jnp.sin(angles))


def convolve(extended, kernel, rows_out, cols_out):
    shaped = extended.reshape(rows_out + 2, cols_out + 2, C, Z)
    moved = jnp.transpose(shaped, (2, 0, 1, 3))
    padded = jnp.pad(moved, ((0, 0), (0, 0), (0, 0), (1, 1)))
    summed = jnp.zeros((C, rows_out * cols_out * Z), jnp.float32)
    for shift_x in range(3):
        for shift_y in range(3):
            for shift_z in range(3):
                window = padded[
                    :,
                    shift_x : shift_x + rows_out,
                    shift_y : shift_y + cols_out,
                    shift_z : shift_z + Z,
                ]
                block = kernel[shift_x, shift_y, :, shift_z * C : (shift_z + 1) * C]
                summed = summed + matmul(block, window.reshape(C, rows_out * cols_out * Z))
    return jnp.transpose(summed.reshape(C, rows_out, cols_out, Z), (1, 2, 0, 3))


def on_device(state_field, conv_first, conv_second, spec_real, spec_imag):
    rows_here = state_field.shape[0]
    cols_here = state_field.shape[1]
    total_x = rows_here * lax.axis_size("gx")
    total_y = cols_here * lax.axis_size("gy")
    row_start = lax.axis_index("gx") * rows_here
    col_start = lax.axis_index("gy") * cols_here
    chan_modes = C * MZ
    width_q = cols_here * chan_modes
    extended = with_halo(state_field, (("gx", 0), ("gy", 1)), 1)
    hidden_field = jax.nn.gelu(
        convolve(extended, conv_first, rows_here, cols_here), approximate=False
    )
    hidden_rim = with_halo(
        hidden_field.reshape(rows_here, cols_here, C * Z), (("gx", 0), ("gy", 1)), 1
    )
    conv_out = convolve(hidden_rim, conv_second, rows_here, cols_here)
    z_cells = jnp.arange(Z, dtype=jnp.int32)
    z_freqs = jnp.arange(MZ, dtype=jnp.int32)
    z_cosine, z_sine = angle_table(z_cells, z_freqs, Z)
    flat_cells = state_field.reshape(rows_here * cols_here * C, Z)
    z_real = matmul(flat_cells, z_cosine).reshape(rows_here, width_q)
    z_imag = -matmul(flat_cells, z_sine).reshape(rows_here, width_q)
    x_freqs = kept_modes(MX, total_x)
    local_x = row_start + jnp.arange(rows_here, dtype=jnp.int32)
    frequency = x_freqs
    cosine, sine_part = angle_table(frequency, local_x, total_x)
    term_real = matmul(cosine, z_real) + matmul(sine_part, z_imag)
    term_imag = matmul(cosine, z_imag) - matmul(sine_part, z_real)
    joined = lax.psum_scatter(
        jnp.concatenate([term_real, term_imag], axis=1), "gx", scatter_dimension=0, tiled=True
    )
    mode_real = joined[:, :width_q]
    mode_imag = joined[:, width_q:]
    kxd_rows = mode_real.shape[0]
    y_real = mode_real.reshape(kxd_rows, cols_here, chan_modes)
    y_imag = mode_imag.reshape(kxd_rows, cols_here, chan_modes)
    y_freqs = kept_modes(MY, total_y)
    local_y = col_start + jnp.arange(cols_here, dtype=jnp.int32)
    frequency = y_freqs
    cosine, sine_part = angle_table(frequency, local_y, total_y)
    term_real = jnp.einsum("my,ayq->maq", cosine, y_real, precision=highest) + jnp.einsum(
        "my,ayq->maq", sine_part, y_imag, precision=highest
    )
    term_imag = jnp.einsum("my,ayq->maq", cosine, y_imag, precision=highest) - jnp.einsum(
        "my,ayq->maq", sine_part, y_real, precision=highest
    )
    owned = lax.psum_scatter(
        jnp.concatenate([term_real, term_imag], axis=2), "gy", scatter_dimension=0, tiled=True
    )
    kyd_rows = owned.shape[0]
    owned_real = owned[..., :chan_modes].reshape(kyd_rows, kxd_rows, C, MZ)
    owned_imag = owned[..., chan_modes:].reshape(kyd_rows, kxd_rows, C, MZ)
    weight_real = spec_real.reshape(kxd_rows, kyd_rows, C, MZ, C)
    weight_imag = spec_imag.reshape(kxd_rows, kyd_rows, C, MZ, C)
    mixed_real = jnp.einsum(
        "baik,abiko->baok", owned_real, weight_real, precision=highest
    ) - jnp.einsum("baik,abiko->baok", owned_imag, weight_imag, precision=highest)
    mixed_imag = jnp.einsum(
        "baik,abiko->baok", owned_real, weight_imag, precision=highest
    ) + jnp.einsum("baik,abiko->baok", owned_imag, weight_real, precision=highest)
    mixed = jnp.concatenate(
        [
            mixed_real.reshape(kyd_rows, kxd_rows, chan_modes),
            mixed_imag.reshape(kyd_rows, kxd_rows, chan_modes),
        ],
        axis=2,
    )
    shard_piece = lax.all_gather(mixed, "gy", axis=0, tiled=True)
    frequency = y_freqs
    cosine, sine_part = angle_table(local_y, frequency, total_y)
    piece_real = shard_piece[..., :chan_modes]
    piece_imag = shard_piece[..., chan_modes:]
    add_real = jnp.einsum("ym,maq->ayq", cosine, piece_real, precision=highest) - jnp.einsum(
        "ym,maq->ayq", sine_part, piece_imag, precision=highest
    )
    add_imag = jnp.einsum("ym,maq->ayq", cosine, piece_imag, precision=highest) + jnp.einsum(
        "ym,maq->ayq", sine_part, piece_real, precision=highest
    )
    returned = jnp.concatenate([add_real, add_imag], axis=2)
    back_real = returned[..., :chan_modes].reshape(kxd_rows, width_q)
    back_imag = returned[..., chan_modes:].reshape(kxd_rows, width_q)
    joined_back = jnp.concatenate([back_real, back_imag], axis=1)
    shard_piece = lax.all_gather(joined_back, "gx", axis=0, tiled=True)
    frequency = x_freqs
    cosine, sine_part = angle_table(local_x, frequency, total_x)
    piece_real = shard_piece[:, :width_q]
    piece_imag = shard_piece[:, width_q:]
    add_real = matmul(cosine, piece_real) - matmul(sine_part, piece_imag)
    add_imag = matmul(cosine, piece_imag) + matmul(sine_part, piece_real)
    gathered = jnp.concatenate([add_real, add_imag], axis=1)
    cell_real = gathered[:, :width_q]
    cell_imag = gathered[:, width_q:]
    scaling = 1.0 / (total_x * total_y * Z)
    factors = jnp.where(z_freqs == 0, 1.0, 2.0).astype(jnp.float32) * scaling
    back_cosine, back_sine = angle_table(z_freqs, z_cells, Z)
    back_cosine = back_cosine * factors[:, None]
    back_sine = back_sine * factors[:, None]
    spectral = matmul(cell_real.reshape(rows_here * cols_here * C, MZ), back_cosine) - matmul(
        cell_imag.reshape(rows_here * cols_here * C, MZ), back_sine
    )
    spectral = spectral.reshape(rows_here, cols_here, C, Z)
    layer_out = jax.nn.gelu(spectral + conv_out, approximate=False)
    return layer_out.reshape(rows_here, cols_here, C * Z)


def solution(mesh):
    in_specs = (P("gx", "gy", None), P(), P(), P("gx", "gy", None, None), P("gx", "gy", None, None))
    out_specs = P("gx", "gy", None)
    return jax.shard_map(
        on_device, mesh=mesh, in_specs=in_specs, out_specs=out_specs, check_vma=False
    )
```

profile of v0, /device:TPU:1, one launch (start us, length us, event | category | flops | bytes accessed | tf_op | source)
XLA Modules:
  0.0 637.4 jit_solution(1770213632262422438)
XLA Ops:
  7.5 8.8 %collective-permute-start.1 = (f32[1,8,2304]{2,1,0:T(8,128)S(1)}, f32[1,8,2304]{2,1,0:T(8,128)S(1)}, u32[]{:S(2)}, u32[]{:S(2)}) collective-permute-start(f32[1,8,2304]{2,1,0:T(8,128)S(1)} %get-tuple-element.75), channel_id=1, source_target_pairs={{16,0},{32,16},{48,32},{64,48},{80,64},{96,80},{112,96},{128,112},... | collective-permute-start | bytes 221192 | tf_op jit(solution)/shard_map/ppermute | solution.py:27
  16.3 1.9 collective-permute-start
  24.9 5.0 collective-permute-start.2
  32.8 10.6 %collective-permute-done.3 = f32[6,1,2304]{2,1,0:T(1,128)S(1)} collective-permute-done((f32[6,1,2304]{2,1,0:T(1,128)S(1)}, f32[6,1,2304]{2,1,0:T(1,128)S(1)}, u32[]{:S(2)}, u32[]{:S(2)}) %collective-permute-start.3) | collective-permute-done | bytes 55328 | tf_op jit(solution)/shard_map/ppermute | solution.py:27
  44.3 1.9 fusion.327
  46.2 4.3 pad_slice_fusion.24
  50.5 3.8 fusion.326
  56.8 2.0 reshape.348
  60.0 2.0 reshape.345
  63.1 2.0 reshape.342
  66.3 2.0 reshape.339
  69.5 2.0 reshape.338
  72.7 2.0 reshape.355
  75.8 2.0 reshape.340
  79.0 2.0 reshape.341
  82.2 2.0 reshape.343
  85.3 2.0 reshape.344
  88.5 2.0 reshape.346
  91.7 2.0 reshape.347
  94.8 2.0 reshape.349
  98.2 2.0 reshape.350
  101.5 2.1 fusion.130
  103.6 2.2 convolution_bitcast_fusion.11
  107.0 2.0 reshape.354
  110.1 2.0 reshape.352
  113.3 2.0 reshape.353
  117.8 1.9 convolution_bitcast_fusion.18
  121.0 2.2 convolution_bitcast_fusion.16
  124.5 2.1 convolution_bitcast_fusion.15
  127.9 2.2 convolution_bitcast_fusion.13
  134.1 1.9 convolution_bitcast_fusion.14
  149.4 1.9 collective-permute-start.4
  151.6 2.4 collective-permute-start.5
  154.1 3.6 collective-permute-done.5
  157.8 8.5 %collective-permute-start.6 = (f32[6,1,2304]{2,1,0:T(1,128)S(1)}, f32[6,1,2304]{2,1,0:T(1,128)S(1)}, u32[]{:S(2)}, u32[]{:S(2)}) collective-permute-start(f32[6,1,2304]{2,1,0:T(1,128)S(1)} %get-tuple-element.69), channel_id=1, source_target_pairs={{0,1},{1,2},{2,3},{3,4},{4,5},{5,6},{6,7},{7,8},{8,9},{9,10},{10,1... | collective-permute-start | bytes 165896 | tf_op jit(solution)/shard_map/ppermute | solution.py:25
  166.3 1.7 collective-permute-start.7
  173.5 4.0 collective-permute-done.7
  178.4 1.9 fusion.325
  180.4 4.3 pad_slice_fusion.6
  184.6 3.8 fusion.324
  190.9 2.0 reshape.377
  194.1 2.0 reshape.374
  197.2 2.0 reshape.371
  200.4 2.0 reshape.368
  203.6 2.0 reshape.367
  206.8 2.0 reshape.384
  210.0 2.0 reshape.369
  213.2 2.0 reshape.370
  216.3 2.0 reshape.372
  219.5 2.0 reshape.373
  222.7 2.0 reshape.375
  225.8 2.0 reshape.376
  229.2 2.0 reshape.378
  232.3 2.0 reshape.379
  236.9 2.1 fusion.102
  241.4 2.0 reshape.383
  244.6 2.0 reshape.381
  247.8 2.0 reshape.382
  280.7 38.4 %all-reduce.7.cloned.1.call-done = f32[32,6912]{1,0:T(8,128)} async-done(((f32[32,6912]{1,0:T(8,128)}), f32[32,6912]{1,0:T(8,128)}) %all-reduce.7.cloned.1.call-update) | async-done | bytes 884752
  319.1 1.7 dynamic-slice_reduce_fusion.1
  323.2 1.8 fusion.19
  325.2 188.3 %all-reduce.9.cloned.1.call-done = f32[32,1,864]{2,0,1:T(8,128)} async-done(((f32[32,1,864]{2,0,1:T(8,128)}), f32[32,1,864]{2,0,1:T(8,128)}) %all-reduce.9.cloned.1.call-update) | async-done | bytes 110608
  515.8 42.2 %all_gather.6 = f32[32,1,864]{2,1,0:T(1,128)S(1)} all-gather(f32[2,1,864]{2,1,0:T(1,128)S(1)} %copy.74), channel_id=1, replica_groups=mesh['gx'=32,'gy'=16] {'gy'}, dimensions={0}, use_global_device_ids=true | all-gather | bytes 117504 | tf_op jit(solution)/shard_map/all_gather | solution.py:136
  559.5 63.2 %all-gather = f32[32,1,6912]{2,1,0:T(1,128)S(1)} all-gather(f32[1,1,6912]{2,1,0:T(1,128)S(1)} %maximum_bitcast_fusion), channel_id=1, replica_groups=mesh['gx'=32,'gy'=16] {'gx'}, dimensions={0}, use_global_device_ids=true | all-gather | bytes 912384 | tf_op jit(solution)/shard_map/all_gather | solution.py:151
  (420 shorter events, 132.9 us)
Async XLA Ops:
  6.5 312.6 %all-reduce.7.cloned.1.call-start = ((), (), s32[]{:S(2)}) async-start(), calls=%async_computation | async-start | bytes 1769472
  7.5 17.3 %collective-permute-start.1 = (f32[1,8,2304]{2,1,0:T(8,128)S(1)}, f32[1,8,2304]{2,1,0:T(8,128)S(1)}, u32[]{:S(2)}, u32[]{:S(2)}) collective-permute-start(f32[1,8,2304]{2,1,0:T(8,128)S(1)} %get-tuple-element.75), channel_id=1, source_target_pairs={{16,0},{32,16},{48,32},{64,48},{80,64},{96,80},{112,96},{128,112},... | collective-permute-start | bytes 221192 | tf_op jit(solution)/shard_map/ppermute | solution.py:27
  16.3 8.5 %collective-permute-start = (f32[1,8,2304]{2,1,0:T(8,128)S(1)}, f32[1,8,2304]{2,1,0:T(8,128)S(1)}, u32[]{:S(2)}, u32[]{:S(2)}) collective-permute-start(f32[1,8,2304]{2,1,0:T(8,128)S(1)} %get-tuple-element.76), channel_id=1, source_target_pairs={{0,16},{16,32},{32,48},{48,64},{64,80},{80,96},{96,112},{112,128},... | collective-permute-start | bytes 221192 | tf_op jit(solution)/shard_map/ppermute | solution.py:25
  24.9 7.9 %collective-permute-start.2 = (f32[6,1,2304]{2,1,0:T(1,128)S(1)}, f32[6,1,2304]{2,1,0:T(1,128)S(1)}, u32[]{:S(2)}, u32[]{:S(2)}) collective-permute-start(f32[6,1,2304]{2,1,0:T(1,128)S(1)} %get-tuple-element.71), channel_id=1, source_target_pairs={{0,1},{1,2},{2,3},{3,4},{4,5},{5,6},{6,7},{7,8},{8,9},{9,10},{10,1... | collective-permute-start | bytes 165896 | tf_op jit(solution)/shard_map/ppermute | solution.py:25
  29.9 13.5 %collective-permute-start.3 = (f32[6,1,2304]{2,1,0:T(1,128)S(1)}, f32[6,1,2304]{2,1,0:T(1,128)S(1)}, u32[]{:S(2)}, u32[]{:S(2)}) collective-permute-start(f32[6,1,2304]{2,1,0:T(1,128)S(1)} %get-tuple-element.72), channel_id=1, source_target_pairs={{1,0},{2,1},{3,2},{4,3},{5,4},{6,5},{7,6},{8,7},{9,8},{10,9},{11,1... | collective-permute-start | bytes 165896 | tf_op jit(solution)/shard_map/ppermute | solution.py:27
  32.2 481.3 %all-reduce.9.cloned.1.call-start = ((), (), s32[]{:S(2)}) async-start(), calls=%async_computation.1 | async-start | bytes 229376
  55.6 3.2 copy-start.42
  58.8 3.2 copy-start.40
  62.0 3.2 copy-start.38
  65.1 3.2 copy-start.36
  68.3 3.2 copy-start.34
  71.5 3.2 copy-start.32
  74.7 3.2 copy-start.30
  77.8 3.2 copy-start.28
  81.0 3.2 copy-start.26
  84.2 3.2 copy-start.24
  87.4 3.2 copy-start.22
  90.5 3.2 copy-start.20
  93.7 3.2 copy-start.18
  96.8 3.3 copy-start.16
  100.5 5.3 copy-start.14
  105.7 3.2 copy-start.12
  109.0 3.2 copy-start.10
  112.1 3.2 copy-start.8
  116.5 3.2 copy-start.6
  120.1 3.1 copy-start.4
  149.3 21.2 %copy-start.100 = (f32[1,2,36,432]{3,1,2,0:T(2,128)S(1)}, f32[1,2,36,432]{3,1,2,0:T(2,128)}, u32[]{:S(2)}) copy-start(f32[1,2,36,432]{3,1,2,0:T(2,128)} %param.8) | copy-start | bytes 373252
  149.4 4.6 collective-permute-start.4
  151.5 20.2 %copy-start.101 = (f32[1,2,36,432]{3,1,2,0:T(2,128)S(1)}, f32[1,2,36,432]{3,1,2,0:T(2,128)}, u32[]{:S(2)}) copy-start(f32[1,2,36,432]{3,1,2,0:T(2,128)} %param.9) | copy-start | bytes 373252
  151.6 6.1 collective-permute-start.5
  157.8 15.7 %collective-permute-start.6 = (f32[6,1,2304]{2,1,0:T(1,128)S(1)}, f32[6,1,2304]{2,1,0:T(1,128)S(1)}, u32[]{:S(2)}, u32[]{:S(2)}) collective-permute-start(f32[6,1,2304]{2,1,0:T(1,128)S(1)} %get-tuple-element.69), channel_id=1, source_target_pairs={{0,1},{1,2},{2,3},{3,4},{4,5},{5,6},{6,7},{7,8},{8,9},{9,10},{10,1... | collective-permute-start | bytes 165896 | tf_op jit(solution)/shard_map/ppermute | solution.py:25
  166.3 11.2 %collective-permute-start.7 = (f32[6,1,2304]{2,1,0:T(1,128)S(1)}, f32[6,1,2304]{2,1,0:T(1,128)S(1)}, u32[]{:S(2)}, u32[]{:S(2)}) collective-permute-start(f32[6,1,2304]{2,1,0:T(1,128)S(1)} %get-tuple-element.70), channel_id=1, source_target_pairs={{1,0},{2,1},{3,2},{4,3},{5,4},{6,5},{7,6},{8,7},{9,8},{10,9},{11,1... | collective-permute-start | bytes 165896 | tf_op jit(solution)/shard_map/ppermute | solution.py:27
  189.7 3.2 copy-start.43
  192.9 3.2 copy-start.41
  196.1 3.2 copy-start.39
  199.2 3.2 copy-start.37
  202.4 3.2 copy-start.35
  205.6 3.2 copy-start.33
  208.8 3.2 copy-start.31
  212.0 3.2 copy-start.29
  215.2 3.2 copy-start.27
  218.3 3.2 copy-start.25
  221.5 3.2 copy-start.23
  224.7 3.2 copy-start.21
  227.8 3.3 copy-start.19
  231.1 3.2 copy-start.17
  235.5 4.7 copy-start.15
  240.2 3.2 copy-start.13
  243.4 3.2 copy-start.11
  246.6 3.2 copy-start.9
  249.7 3.6 copy-start.7
  253.4 3.7 copy-start.5
  257.0 3.6 copy-start.3
  260.7 3.6 copy-start.1
  279.0 44.1 %copy-start.58 = (f32[36,2048]{1,0:T(8,128)S(1)}, f32[36,2048]{1,0:T(8,128)}, u32[]{:S(2)}) copy-start(f32[36,2048]{1,0:T(8,128)} %convolution_bitcast_fusion.3) | copy-start | bytes 884740
  279.0 44.1 %copy-start.59 = (f32[36,2048]{1,0:T(8,128)S(1)}, f32[36,2048]{1,0:T(8,128)}, u32[]{:S(2)}) copy-start(f32[36,2048]{1,0:T(8,128)} %convolution_bitcast_fusion.2) | copy-start | bytes 884740
  279.0 44.1 %copy-start.60 = (f32[36,2048]{1,0:T(8,128)S(1)}, f32[36,2048]{1,0:T(8,128)}, u32[]{:S(2)}) copy-start(f32[36,2048]{1,0:T(8,128)} %convolution_bitcast_fusion) | copy-start | bytes 884740
  279.4 43.7 %copy-start.51 = (f32[36,2048]{1,0:T(8,128)S(1)}, f32[36,2048]{1,0:T(8,128)}, u32[]{:S(2)}) copy-start(f32[36,2048]{1,0:T(8,128)} %reshape.384) | copy-start | bytes 884740
  279.4 43.7 %copy-start.53 = (f32[36,2048]{1,0:T(8,128)S(1)}, f32[36,2048]{1,0:T(8,128)}, u32[]{:S(2)}) copy-start(f32[36,2048]{1,0:T(8,128)} %convolution_bitcast_fusion.1) | copy-start | bytes 884740
  279.5 43.7 %copy-start.54 = (f32[36,2048]{1,0:T(8,128)S(1)}, f32[36,2048]{1,0:T(8,128)}, u32[]{:S(2)}) copy-start(f32[36,2048]{1,0:T(8,128)} %convolution_bitcast_fusion.8) | copy-start | bytes 884740
  279.5 43.7 %copy-start.55 = (f32[36,2048]{1,0:T(8,128)S(1)}, f32[36,2048]{1,0:T(8,128)}, u32[]{:S(2)}) copy-start(f32[36,2048]{1,0:T(8,128)} %convolution_bitcast_fusion.6) | copy-start | bytes 884740
  279.5 43.7 %copy-start.56 = (f32[36,2048]{1,0:T(8,128)S(1)}, f32[36,2048]{1,0:T(8,128)}, u32[]{:S(2)}) copy-start(f32[36,2048]{1,0:T(8,128)} %convolution_bitcast_fusion.5) | copy-start | bytes 884740
  324.9 189.7 %copy-start.46 = (f32[2,36,12,36]{3,2,0,1:T(8,128)S(1)}, f32[2,36,12,36]{3,2,0,1:T(8,128)}, u32[]{:S(2)}) copy-start(f32[2,36,12,36]{3,2,0,1:T(8,128)} %reshape.325) | copy-start | bytes 373252
  324.9 189.7 %copy-start.47 = (f32[2,36,12,36]{3,2,0,1:T(8,128)S(1)}, f32[2,36,12,36]{3,2,0,1:T(8,128)}, u32[]{:S(2)}) copy-start(f32[2,36,12,36]{3,2,0,1:T(8,128)} %reshape.327) | copy-start | bytes 373252
  (48 other events, 66.0 us)
Sparse Core Ops, SparseCore 0:
  32.3 286.7 all-reduce.6
  323.2 190.2 all-reduce.8
where the time goes:
time: 644 us; the launch traced here: 637 us
  waiting for transfers between devices  245 us (38%)
  local copies, waits for them, and re-layouts  174 us (27%)
  blocking collectives  105 us (16%)
  matrix products  58.9 us (9%)
  starting transfers between devices  32 us (5%)
  between operations  15.8 us (2%)
    unnamed x4, waiting for transfers between devices  227 us
    reshape x54, local copies, waits for them, and re-layouts, convolve(): summed = summed + matmul(block, window.reshape(C, rows_out * cols_out * Z))  82.9 us
    slice x60, local copies, waits for them, and re-layouts, convolve(): padded[:, shift_x:shift_x + rows_out, shift_y:shift_y + cols_out, shift_z...  72 us
    all_gather x1, blocking collectives, on_device(): shard_piece = lax.all_gather(joined_back, 'gx', axis=0, tiled=True)  63.2 us
    dot_general x66, matrix products, matmul(): return jnp.dot(left, right, precision=highest)  56.6 us
    all_gather x1, blocking collectives, on_device(): shard_piece = lax.all_gather(mixed, 'gy', axis=0, tiled=True)  42.2 us
    ppermute x4, waiting for transfers between devices, with_halo(): lax.ppermute(head, axis, [((i + 1) % count, i) for i in range(ends)])  18.2 us
    ppermute x4, starting transfers between devices, with_halo(): lax.ppermute(tail, axis, [(i, (i + 1) % count) for i in range(ends)])  17.3 us
  transfers between devices with their start and end apart: 10, of which 5 were waited for; matrix products, arithmetic and copies ran while one was open for 35% of the time, Pallas kernels for 0%

commit v1 on v0

v1 whole, which is shorter than its diff:
```python
import jax
import jax.numpy as jnp
import numpy as np
from jax import lax
from jax.experimental import pallas as pl
from jax.experimental.pallas import tpu as pltpu
from jax.sharding import PartitionSpec as P

C = 36
Z = 64
MZ = 12
X = 128
Y = 128
GX = 32
GY = 16
NX = 4
NY = 8
GROUP = 8
KB = 112
F32 = jnp.float32
BF16 = jnp.bfloat16
MESH = pl.DeviceIdType.MESH


def halves(table):
    high = table.astype(jnp.bfloat16)
    low = (table - high.astype(np.float64)).astype(jnp.bfloat16)
    return high, low


def stacked(table, pad=0):
    high, low = halves(table)
    parts = [high, high, low]
    if pad:
        parts.append(np.zeros(high.shape[:-1] + (pad,), high.dtype))
    return np.concatenate(parts, axis=-1)


def tables():
    r = np.arange(MZ)
    z = np.arange(Z)
    zr = 2 * np.pi * np.outer(z, r) / Z
    forward = np.zeros((704, 256))
    backward = np.zeros((2, 256, 640))
    weight = np.where(r == 0, 1.0, 2.0) / (X * Y * Z)
    for c in range(9):
        rows = slice(64 + c * Z, 64 + c * Z + Z)
        forward[rows, c * MZ : c * MZ + MZ] = np.cos(zr)
        forward[rows, 128 + c * MZ : 128 + c * MZ + MZ] = -np.sin(zr)
        for e in range(2):
            cols = slice(64 * e + c * Z, 64 * e + c * Z + Z)
            backward[e, c * MZ : c * MZ + MZ, cols] = (np.cos(zr) * weight).T
            backward[e, 128 + c * MZ : 128 + c * MZ + MZ, cols] = -(np.sin(zr) * weight).T
    freq = np.where(np.arange(32) < 16, np.arange(32), np.arange(32) + 96)

    def pair(first, second):
        angle = 2 * np.pi * (np.outer(first, second) % 128) / 128
        return np.concatenate([np.cos(angle), np.sin(angle)], axis=0)

    xs = [np.arange(32) + 32 * g for g in range(4)]
    ys = [np.arange(NY) + NY * g for g in range(GY)]
    d1 = stacked(np.stack([pair(freq, v) for v in xs]))
    d2 = stacked(np.stack([pair(freq, v) for v in ys]), 8)
    d4 = stacked(np.stack([pair(v, freq) for v in ys]))
    d5 = stacked(np.stack([pair(v, freq) for v in xs]))
    mask = np.zeros((4, 40, 128), np.float32)
    spread = np.zeros((128, 512))
    order = np.zeros((512, 512))
    for c in range(C):
        mask[c // 9, c, (c % 9) * MZ : (c % 9) * MZ + MZ] = 1
    for c in range(9):
        for k in range(MZ):
            spread[c * MZ + k, k * C : k * C + C] = 1
    for k in range(MZ):
        for o in range(C):
            order[k * C + o, (o // 9) * 128 + (o % 9) * MZ + k] = 1
    return (
        np.stack(halves(forward)),
        d1,
        d2,
        d4,
        d5,
        mask,
        spread.astype(jnp.bfloat16),
        order.astype(jnp.bfloat16),
        np.stack(halves(backward), axis=1),
    )


def split(value):
    high = value.astype(BF16)
    low = (value - high.astype(F32)).astype(BF16)
    return high, low


def split32(value):
    high = value.astype(BF16).astype(F32)
    return high, value - high


def dot(left, right):
    return jnp.dot(left, right, preferred_element_type=F32)


def gelu(value):
    return 0.5 * value * (1.0 + lax.erf(value * 0.7071067811865476))


def kernel(
    state_hbm, wf_hbm, ws_hbm, sr_hbm, si_hbm,
    fz_hbm, d1_hbm, d2_hbm, d4_hbm, d5_hbm, mk_hbm, ex_hbm, pm_hbm, fi_hbm,
    out_ref,
    st, wf, ws, sr, si, fz, d1, d2, d4, d5, mk, ex, pm, fi,
    s1, r1, s2, r2, s3, r3, s4, r4, s5, r5, s6, r6,
    tt, m8, wst1, wst2, cc, stage, ubh, ubl, hid, stage2, ub2h, ub2l, ct, n2, co,
    load_sem, send_sem, recv_sem, halo_send, halo_recv,
):
    i = lax.axis_index("gx")
    j = lax.axis_index("gy")
    a = i // GROUP
    l = i % GROUP

    sources = [
        (state_hbm, st), (fz_hbm, fz), (d1_hbm.at[a], d1), (d2_hbm.at[j], d2), (wf_hbm, wf),
        (ws_hbm, ws), (sr_hbm.at[0], sr), (si_hbm.at[0], si), (mk_hbm, mk), (ex_hbm, ex),
        (pm_hbm, pm), (d4_hbm.at[j], d4), (d5_hbm.at[a], d5), (fi_hbm, fi),
    ]
    loads = [pltpu.make_async_copy(src, dst, load_sem.at[n]) for n, (src, dst) in enumerate(sources)]
    for load in loads:
        load.start()
    (l_st, l_fz, l_d1, l_d2, l_wf, l_ws, l_sr, l_si, l_mk, l_ex, l_pm, l_d4, l_d5, l_fi) = loads

    barrier = pltpu.get_barrier_semaphore()

    @pl.loop(1, GX)
    def _(s):
        pl.semaphore_signal(barrier, inc=1, device_id=((i + s) % GX, j), device_id_type=MESH)

    @pl.loop(1, GY)
    def _(s):
        pl.semaphore_signal(barrier, inc=1, device_id=(i, (j + s) % GY), device_id_type=MESH)

    def remote(src, dst, stage_no, device):
        return pltpu.make_async_remote_copy(
            src_ref=src, dst_ref=dst, send_sem=send_sem.at[stage_no], recv_sem=recv_sem.at[stage_no],
            device_id=device, device_id_type=MESH,
        )

    def rows(start, size):
        return pl.ds(pl.multiple_of(start, 8), size)

    def wait_recv(buffer, count, stage_no):
        part = buffer.at[pl.ds(0, count)]
        pltpu.make_async_copy(part, part, recv_sem.at[stage_no]).wait()

    def wait_send(buffer, count, stage_no):
        part = buffer.at[pl.ds(0, count)]
        pltpu.make_async_copy(part, part, send_sem.at[stage_no]).wait()

    lane = lax.broadcasted_iota(jnp.int32, (1, 128), 1)
    first_half = lane < 64

    cc[...] = jnp.zeros_like(cc)
    l_st.wait()
    t2 = tt.reshape(8 * 12 * 24, 128)
    for x in range(NX):
        for m in range(18):
            t2[pl.ds(((x + 2) * 12 + 2) * 24 + m, 8, stride=24), :] = st[x, :, m * 128 : (m + 1) * 128]
    l_fz.wait()
    field = st[...].reshape(NX * NY, C * Z)
    for e in range(2):
        left = jnp.concatenate([field[:, h * 1152 + e * 512 : h * 1152 + e * 512 + 640] for h in range(2)], axis=0)
        high, low = split(left)
        fh = fz[0, 64 * (1 - e) : 64 * (1 - e) + 640, :]
        fl = fz[1, 64 * (1 - e) : 64 * (1 - e) + 640, :]
        res = dot(high, fh) + dot(low, fh) + dot(high, fl)
        for h in range(2):
            for part in range(2):
                for x in range(NX):
                    s1[pl.ds(x * 8 + part * 4 + 2 * h + e, 8, stride=32), :] = res[
                        h * 32 + x * 8 : h * 32 + x * 8 + 8, part * 128 : part * 128 + 128
                    ]
    pl.semaphore_wait(barrier, GX - 1 + GY - 1)

    @pl.loop(1, GROUP)
    def _(s):
        t = (l + s) % GROUP
        remote(s1.at[rows(t * 32, 32)], r1.at[rows(l * 32, 32)], 0, (a * GROUP + t, j)).start()

    r1[rows(l * 32, 32), :] = s1[rows(l * 32, 32), :]

    def halo(n, src, dst, device):
        return pltpu.make_async_remote_copy(
            src_ref=src, dst_ref=dst, send_sem=halo_send.at[n], recv_sem=halo_recv.at[n],
            device_id=device, device_id_type=MESH,
        )

    down_y = halo(0, tt.at[2:6, 2:4], tt.at[2:6, 10:12], (i, (j + GY - 1) % GY))
    up_y = halo(1, tt.at[2:6, 8:10], tt.at[2:6, 0:2], (i, (j + 1) % GY))
    down_x = halo(2, tt.at[2:4], tt.at[6:8], ((i + GX - 1) % GX, j))
    up_x = halo(3, tt.at[4:6], tt.at[0:2], ((i + 1) % GX, j))

    @pl.when(j > 0)
    def _():
        down_y.start()

    @pl.when(j < GY - 1)
    def _():
        up_y.start()

    @pl.when(j == 0)
    def _():
        tt[2:6, 0:2] = jnp.zeros((4, 2, 24, 128), F32)

    @pl.when(j == GY - 1)
    def _():
        tt[2:6, 10:12] = jnp.zeros((4, 2, 24, 128), F32)

    @pl.when(i == 0)
    def _():
        tt[0:2] = jnp.zeros((2, 12, 24, 128), F32)

    @pl.when(i == GX - 1)
    def _():
        tt[6:8] = jnp.zeros((2, 12, 24, 128), F32)

    def filters(src, scratch):
        scratch[...] = jnp.zeros_like(scratch)
        for tap_x in range(3):
            for tap_y in range(3):
                tap = tap_x * 3 + tap_y
                high, low = split32(src[tap_x, tap_y])
                scratch[0:36, tap * KB : tap * KB + 108] = high
                scratch[40:76, tap * KB : tap * KB + 108] = low

    l_wf.wait()
    filters(wf, wst1)

    wait_recv(r1, 7 * 32, 0)
    l_d1.wait()

    def gathered(buffer):
        return jnp.concatenate([buffer[pl.ds(k, 32, stride=8), :] for k in range(8)], axis=1)

    def tripled(value):
        high, low = split(value)
        return jnp.concatenate([high, low, high], axis=0)

    def combine(res, count, sign):
        top, bottom = res[:count], res[count:]
        real = top[:, :512] + sign * bottom[:, 512:]
        imag = top[:, 512:] - sign * bottom[:, :512]
        return real, imag

    def scatter_rows(buffer, real, imag, count):
        for k in range(4):
            buffer[pl.ds(k, count, stride=8), :] = real[:, k * 128 : k * 128 + 128]
            buffer[pl.ds(k + 4, count, stride=8), :] = imag[:, k * 128 : k * 128 + 128]

    res = dot(d1[...], tripled(gathered(r1)))
    real, imag = combine(res, 32, 1.0)
    scatter_rows(s2, real, imag, 32)

    @pl.loop(1, GX)
    def _(s):
        t = (i + s) % GX
        remote(s2.at[rows(t * 8, 8)], r2.at[rows(i * 8, 8)], 1, (t, j)).start()

    r2[rows(i * 8, 8), :] = s2[rows(i * 8, 8), :]
    l_ws.wait()
    filters(ws, wst2)

    wait_recv(r2, 31 * 8, 1)
    l_d2.wait()
    summed = []
    for k in range(8):
        total = r2[pl.ds(k, 8, stride=8), :]
        for g in range(1, 4):
            total = total + r2[pl.ds(g * 64 + k, 8, stride=8), :]
        summed.append(total)
    high, low = split32(jnp.concatenate(summed, axis=1))
    right = jnp.concatenate([high, low, high, jnp.zeros_like(high)], axis=0).astype(BF16)
    real, imag = combine(dot(d2[...], right), 32, 1.0)
    scatter_rows(s3, real, imag, 32)

    @pl.loop(1, GY)
    def _(s):
        t = (j + s) % GY
        remote(s3.at[rows(t * 16, 16)], r3.at[rows(j * 16, 16)], 2, (i, t)).start()

    r3[rows(j * 16, 16), :] = s3[rows(j * 16, 16), :]

    @pl.when(j > 0)
    def _():
        up_y.wait_recv()

    @pl.when(j < GY - 1)
    def _():
        down_y.wait_recv()

    @pl.when(i > 0)
    def _():
        down_x.start()

    @pl.when(i < GX - 1)
    def _():
        up_x.start()

    wait_recv(r3, 15 * 16, 2)
    total = r3[0:16, :]
    for n in range(1, GY):
        total = total + r3[n * 16 : n * 16 + 16, :]
    for load in (l_mk, l_ex, l_sr, l_si, l_pm):
        load.wait()
    placed = []
    for q in range(2):
        for part in range(2):
            acc = None
            for g in range(4):
                n = q * 8 + part * 4 + g
                term = total[n : n + 1, :] * mk[g]
                acc = term if acc is None else acc + term
            placed.append(acc)
    high, low = split(jnp.concatenate(placed, axis=0))
    wide = dot(high, ex[...]) + dot(low, ex[...])
    m8[...] = jnp.zeros_like(m8)
    for q in range(2):
        c_re = wide[q * 80 : q * 80 + 36, :432]
        c_im = wide[q * 80 + 40 : q * 80 + 76, :432]
        m8[2 * q : 2 * q + 1, 0:432] = jnp.sum(c_re * sr[q] - c_im * si[q], axis=0, keepdims=True)
        m8[2 * q + 1 : 2 * q + 2, 0:432] = jnp.sum(c_re * si[q] + c_im * sr[q], axis=0, keepdims=True)
    high, low = split32(m8[...])
    moved = dot(jnp.concatenate([high, low], axis=0).astype(BF16), pm[...])
    mixed = moved[0:8] + moved[8:16]
    for g in range(4):
        s4[pl.ds(g, 4, stride=4), :] = mixed[0:4, g * 128 : g * 128 + 128]

    @pl.loop(1, GY)
    def _(s):
        t = (j + s) % GY
        remote(s4, r4.at[rows(j * 16, 16)], 3, (i, t)).start()

    r4[rows(j * 16, 16), :] = s4[...]

    @pl.when(i > 0)
    def _():
        up_x.wait_recv()

    @pl.when(i < GX - 1)
    def _():
        down_x.wait_recv()

    z_of = lane % 64

    def shifted(value, d):
        if d == 0:
            return jnp.where(z_of == 0, 0.0, pltpu.roll(value, 1, axis=1))
        if d == 2:
            return jnp.where(z_of == 63, 0.0, pltpu.roll(value, 127, axis=1))
        return value

    def columns(value, buffer, base):
        for d in range(3):
            buffer[base + d * 36 : base + d * 36 + 36, :] = shifted(value, d)[0:36]
        return split(buffer[base : base + KB, :])

    stage[...] = jnp.zeros_like(stage)
    stage2[...] = jnp.zeros_like(stage2)

    @pl.loop(0, 8)
    def _(x):
        for u in range(7):
            near = t2[rows((x * 12 + u) * 24, 24), :]
            far = t2[rows((x * 12 + u + 5) * 24, 24), :]
            even = jnp.where(first_half, near, pltpu.roll(far, 64, axis=1))
            odd = jnp.where(first_half, pltpu.roll(near, 64, axis=1), far)
            cc[pl.ds(u * 40, 18, stride=2), :] = even[0:18]
            cc[pl.ds(u * 40 + 1, 18, stride=2), :] = odd[0:18]
            high, low = columns(cc[u * 40 : u * 40 + 40, :], stage, u * KB)
            for b in range(3):
                v = u - b
                if 0 <= v < 5:
                    place = pl.ds(pl.multiple_of(x * 336 + b * KB, 16), KB)
                    ubh[place, v * 128 : v * 128 + 128] = high
                    ubl[place, v * 128 : v * 128 + 128] = low

    w1 = wst1[...].astype(BF16)
    wide_lane = lax.broadcasted_iota(jnp.int32, (1, 640), 1)
    keep_y = jnp.where((wide_lane < 64) & (j == 0), 0.0, 1.0) * jnp.where(
        (wide_lane >= 576) & (j == GY - 1), 0.0, 1.0
    )

    @pl.loop(0, 6)
    def _(x):
        place = pl.ds(pl.multiple_of(x * 336, 16), 1008)
        res = dot(w1, ubh[place, :])
        value = res[0:40] + res[40:80] + dot(w1[0:40], ubl[place, :])
        outside = ((x == 0) & (i == 0)) | ((x == 5) & (i == GX - 1))
        keep = keep_y * jnp.where(outside, 0.0, 1.0)
        hid[rows(x * 40, 40), :] = gelu(value) * keep

    wait_recv(r4, 15 * 16, 3)
    l_d4.wait()
    real, imag = combine(dot(d4[...], tripled(gathered(r4))), 8, -1.0)
    scatter_rows(s5, real, imag, 8)

    @pl.loop(1, GX)
    def _(s):
        t = (i + s) % GX
        remote(s5.at[rows((t % GROUP) * 8, 8)], r5.at[rows(i * 8, 8)], 4, (t, j)).start()

    r5[rows(i * 8, 8), :] = s5[rows(l * 8, 8), :]

    @pl.loop(0, 6)
    def _(x):
        pairs = [hid[rows(x * 40, 40), v * 128 : v * 128 + 128] for v in range(5)]
        units = [(pairs[n], [(b, n - b) for b in range(3) if 0 <= n - b < 3]) for n in range(5)]
        units.append((jnp.where(first_half, pairs[3], pltpu.roll(pairs[4], 64, axis=1)), [(0, 3)]))
        units.append((jnp.where(first_half, pairs[4], pairs[0]), [(1, 3)]))
        units.append((jnp.where(first_half, pltpu.roll(pairs[0], 64, axis=1), pairs[1]), [(2, 3)]))
        for n, (value, places) in enumerate(units):
            high, low = columns(value, stage2, n * KB)
            for b, v in places:
                place = pl.ds(pl.multiple_of(x * 336 + b * KB, 16), KB)
                ub2h[place, v * 128 : v * 128 + 128] = high
                ub2l[place, v * 128 : v * 128 + 128] = low

    wait_recv(r5, 31 * 8, 4)
    l_d5.wait()
    real, imag = combine(dot(d5[...], tripled(gathered(r5))), 32, -1.0)
    scatter_rows(s6, real, imag, 32)

    @pl.loop(1, GROUP)
    def _(s):
        t = (l + s) % GROUP
        remote(s6.at[rows(t * 32, 32)], r6.at[rows(l * 32, 32)], 5, (a * GROUP + t, j)).start()

    r6[rows(l * 32, 32), :] = s6[rows(l * 32, 32), :]

    w2 = wst2[...].astype(BF16)

    @pl.loop(0, NX)
    def _(x):
        place = pl.ds(pl.multiple_of(x * 336, 16), 1008)
        res = dot(w2, ub2h[place, :])
        value = res[0:40] + res[40:80] + dot(w2[0:40], ub2l[place, :])
        for v in range(4):
            ct[v * 40 : v * 40 + 40, :] = value[:, v * 128 : v * 128 + 128]
        for v in range(4):
            even = ct[pl.ds(v * 40, 18, stride=2), :]
            odd = ct[pl.ds(v * 40 + 1, 18, stride=2), :]
            near = jnp.where(first_half, even, pltpu.roll(odd, 64, axis=1))
            far = jnp.where(first_half, pltpu.roll(even, 64, axis=1), odd)
            y_near, y_far = (v, v + 5) if v < 3 else (3, 4)
            n2[y_near * 24 : y_near * 24 + 18, :] = near
            n2[y_far * 24 : y_far * 24 + 18, :] = far
        for m in range(18):
            co[rows(x * 8, 8), m * 128 : m * 128 + 128] = n2[pl.ds(m, 8, stride=24), :]

    wait_recv(r6, 7 * 32, 5)
    l_fi.wait()
    results = []
    for e in range(2):
        left = jnp.concatenate(
            [
                jnp.concatenate(
                    [
                        jnp.concatenate(
                            [r6[pl.ds(x * 8 + part * 4 + 2 * h + e, 8, stride=32), :] for x in range(NX)], axis=0
                        )
                        for part in range(2)
                    ],
                    axis=1,
                )
                for h in range(2)
            ],
            axis=0,
        )
        high, low = split(left)
        results.append(dot(high, fi[e, 0]) + dot(low, fi[e, 0]) + dot(high, fi[e, 1]))
    for h in range(2):
        one, two = results[0][h * 32 : h * 32 + 32], results[1][h * 32 : h * 32 + 32]
        spectral = jnp.concatenate([one[:, :512], one[:, 512:] + two[:, :128], two[:, 128:]], axis=1)
        full = spectral + co[:, h * 1152 : h * 1152 + 1152]
        for x in range(NX):
            out_ref[x, :, h * 1152 : h * 1152 + 1152] = full[x * 8 : x * 8 + 8]

    wait_send(s1, 7 * 32, 0)
    wait_send(s2, 31 * 8, 1)
    wait_send(s3, 15 * 16, 2)
    wait_send(r4, 15 * 16, 3)
    wait_send(r5, 31 * 8, 4)
    wait_send(s6, 7 * 32, 5)

    @pl.when(j > 0)
    def _():
        down_y.wait_send()

    @pl.when(j < GY - 1)
    def _():
        up_y.wait_send()

    @pl.when(i > 0)
    def _():
        down_x.wait_send()

    @pl.when(i < GX - 1)
    def _():
        up_x.wait_send()


def on_device(state_field, conv_first, conv_second, spec_real, spec_imag):
    constants = [jnp.asarray(t) for t in tables()]
    vm = pltpu.VMEM
    scratch = [
        vm((NX, NY, C * Z), F32), vm((3, 3, C, 3 * C), F32), vm((3, 3, C, 3 * C), F32),
        vm((2, C, MZ * C), F32), vm((2, C, MZ * C), F32),
        vm((2, 704, 256), BF16), vm((64, 96), BF16), vm((64, 32), BF16), vm((16, 96), BF16), vm((64, 96), BF16),
        vm((4, 40, 128), F32), vm((128, 512), BF16), vm((512, 512), BF16), vm((2, 2, 256, 640), BF16),
        vm((256, 128), F32), vm((256, 128), F32), vm((256, 128), F32), vm((256, 128), F32),
        vm((256, 128), F32), vm((256, 128), F32), vm((16, 128), F32), vm((256, 128), F32),
        vm((64, 128), F32), vm((256, 128), F32), vm((256, 128), F32), vm((256, 128), F32),
        vm((8, 12, 24, 128), F32), vm((8, 512), F32), vm((80, 9 * KB), F32), vm((80, 9 * KB), F32),
        vm((280, 128), F32), vm((7 * KB, 128), F32), vm((8 * 336, 640), BF16), vm((8 * 336, 640), BF16),
        vm((240, 640), F32), vm((8 * KB, 128), F32), vm((6 * 336, 512), BF16), vm((6 * 336, 512), BF16),
        vm((160, 128), F32), vm((192, 128), F32), vm((32, C * Z), F32),
        pltpu.SemaphoreType.DMA((14,)), pltpu.SemaphoreType.DMA((6,)), pltpu.SemaphoreType.DMA((6,)),
        pltpu.SemaphoreType.DMA((4,)), pltpu.SemaphoreType.DMA((4,)),
    ]
    before = pl.pallas_call(
        kernel,
        out_shape=jax.ShapeDtypeStruct((NX, NY, C * Z), F32),
        in_specs=[pl.BlockSpec(memory_space=pl.ANY)] * (5 + len(constants)),
        out_specs=pl.BlockSpec(memory_space=pltpu.VMEM),
        scratch_shapes=scratch,
        compiler_params=pltpu.CompilerParams(
            collective_id=0, has_side_effects=True, vmem_limit_bytes=40 * 1024 * 1024
        ),
    )(state_field, conv_first, conv_second, spec_real, spec_imag, *constants)
    return jax.nn.gelu(before, approximate=False)


def solution(mesh):
    in_specs = (P("gx", "gy", None), P(), P(), P("gx", "gy", None, None), P("gx", "gy", None, None))
    return jax.shard_map(
        on_device, mesh=mesh, in_specs=in_specs, out_specs=P("gx", "gy", None), check_vma=False
    )
```

time: 644 us -> 86.5 us (0.13)
  waiting for transfers between devices: 245 us -> 0 us
  local copies, waits for them, and re-layouts: 174 us -> 13.4 us
  blocking collectives: 105 us -> 0 us
  Pallas kernels: 0 us -> 71.1 us
  matrix products: 58.9 us -> 0 us
  starting transfers between devices: 32 us -> 0 us
  between operations: 15.8 us -> 0.04 us
    unnamed x4 -> x0, waiting for transfers between devices: 227 us -> none
    all_gather x2 -> x0, blocking collectives: 105 us -> none  [the longest x1 63.2 us: on_device(): shard_piece = lax.all_gather(joined_back, 'gx', axis=0, tiled=True)]
    reshape x69 -> x0, local copies, waits for them, and re-layouts: 88.3 us -> none  [the longest x54 82.9 us: convolve(): summed = summed + matmul(block, window.reshape(C, rows_out * cols_out * Z))]
    slice x69 -> x0, local copies, waits for them, and re-layouts: 76.1 us -> none  [the longest x60 72 us: convolve(): padded[:, shift_x:shift_x + rows_out, shift_y:shift_y + cols_out, shift_z...]
    pallas_call x0 -> x1, Pallas kernels: none -> 71.1 us  [on_device(): pl.pallas_call(kernel, out_shape=jax.ShapeDtypeStruct((NX, NY, C * Z), F3...]
    dot_general x74 -> x0, matrix products: 58.9 us -> none  [the longest x66 56.6 us: matmul(): return jnp.dot(left, right, precision=highest)]
    ppermute x8 -> x0, starting transfers between devices: 31.5 us -> none  [the longest x4 17.3 us: with_halo(): lax.ppermute(tail, axis, [(i, (i + 1) % count) for i in range(ends)])]
    ppermute x8 -> x0, waiting for transfers between devices: 18.2 us -> none  [the longest x4 18.2 us: with_halo(): lax.ppermute(head, axis, [((i + 1) % count, i) for i in range(ends)])]
  transfers between devices with their start and end apart: 10 -> 0, of which waited for: 5 -> 0; matrix products, arithmetic and copies ran while one was open for 35% -> 0% of each run, Pallas kernels for 0% -> 0%
where the time goes in v1:
time: 86.5 us; the launch traced here: 85.9 us
  Pallas kernels  71.1 us (82%)
  local copies, waits for them, and re-layouts  13.4 us (15%)
  other arithmetic  1.35 us (2%)
    pallas_call x1, Pallas kernels, on_device(): pl.pallas_call(kernel, out_shape=jax.ShapeDtypeStruct((NX, NY, C * Z), F3...  71.1 us
    unnamed x26, local copies, waits for them, and re-layouts  13.4 us

profile of v1, /device:TPU:1, one launch (start us, length us, event | category | flops | bytes accessed | tf_op | source)
XLA Modules:
  0.0 85.9 jit_solution(16089377253139046448)
XLA Ops:
  0.0 0.9 %copy.15.sr_hbm = f32[1,2,36,432]{3,2,1,0:T(8,128)S(1)} copy(f32[1,2,36,432]{3,1,2,0:T(2,128)} %param.17) | data formatting | bytes 248832 | tf_op args[3]
  0.9 0.9 %copy.16.si_hbm = f32[1,2,36,432]{3,2,1,0:T(8,128)S(1)} copy(f32[1,2,36,432]{3,1,2,0:T(2,128)} %param.18) | data formatting | bytes 248832 | tf_op args[4]
  1.9 0.0 copy-start
  1.9 1.3 %copy-done = bf16[2,2,256,640]{3,2,1,0:T(8,128)(2,1)S(1)} copy-done((bf16[2,2,256,640]{3,2,1,0:T(8,128)(2,1)S(1)}, bf16[2,2,256,640]{3,2,1,0:T(8,128)(2,1)}, u32[]{:S(2)}) %copy-start) | copy-done | bytes 1310744
  3.2 0.0 copy-start.1
  3.2 1.1 %copy-done.1 = bf16[2,704,256]{2,1,0:T(8,128)(2,1)S(1)} copy-done((bf16[2,704,256]{2,1,0:T(8,128)(2,1)S(1)}, bf16[2,704,256]{2,1,0:T(8,128)(2,1)}, u32[]{:S(2)}) %copy-start.1) | copy-done | bytes 720920
  4.3 0.0 copy-start.2
  4.3 1.0 %copy-done.2 = bf16[512,512]{1,0:T(8,128)(2,1)S(1)} copy-done((bf16[512,512]{1,0:T(8,128)(2,1)S(1)}, bf16[512,512]{1,0:T(8,128)(2,1)}, u32[]{:S(2)}) %copy-start.2) | copy-done | bytes 524312
  5.4 0.0 copy-start.3
  5.4 1.0 %copy-done.3 = f32[4,8,2304]{2,1,0:T(8,128)S(1)} copy-done((f32[4,8,2304]{2,1,0:T(8,128)S(1)}, f32[4,8,2304]{2,1,0:T(8,128)}, u32[]{:S(2)}) %copy-start.3) | copy-done | bytes 294936
  6.3 0.0 copy-start.4
  6.3 0.9 %copy-done.4 = bf16[16,64,32]{2,1,0:T(8,128)(2,1)S(1)} copy-done((bf16[16,64,32]{2,1,0:T(8,128)(2,1)S(1)}, bf16[16,64,32]{2,1,0:T(8,128)(2,1)}, u32[]{:S(2)}) %copy-start.4) | copy-done | bytes 65560
  7.3 0.0 copy-start.5
  7.3 0.9 %copy-done.5 = f32[3,3,36,108]{3,2,1,0:T(8,128)S(1)} copy-done((f32[3,3,36,108]{3,2,1,0:T(8,128)S(1)}, f32[3,3,36,108]{3,2,1,0:T(8,128)}, u32[]{:S(2)}) %copy-start.5) | copy-done | bytes 139992
  8.2 0.0 copy-start.6
  8.2 0.9 %copy-done.6 = f32[3,3,36,108]{3,2,1,0:T(8,128)S(1)} copy-done((f32[3,3,36,108]{3,2,1,0:T(8,128)S(1)}, f32[3,3,36,108]{3,2,1,0:T(8,128)}, u32[]{:S(2)}) %copy-start.6) | copy-done | bytes 139992
  9.1 0.0 copy-start.7
  9.1 0.9 %copy-done.7 = bf16[128,512]{1,0:T(8,128)(2,1)S(1)} copy-done((bf16[128,512]{1,0:T(8,128)(2,1)S(1)}, bf16[128,512]{1,0:T(8,128)(2,1)}, u32[]{:S(2)}) %copy-start.7) | copy-done | bytes 131096
  10.0 0.0 copy-start.8
  10.0 0.9 %copy-done.8 = f32[4,40,128]{2,1,0:T(8,128)S(1)} copy-done((f32[4,40,128]{2,1,0:T(8,128)S(1)}, f32[4,40,128]{2,1,0:T(8,128)}, u32[]{:S(2)}) %copy-start.8) | copy-done | bytes 81944
  10.9 0.0 copy-start.9
  10.9 0.8 copy-done.9
  11.8 0.0 copy-start.10
  11.8 0.8 copy-done.10
  12.6 0.0 copy-start.11
  12.6 0.8 copy-done.11
  13.4 71.1 %shard_map.136 = f32[4,8,2304]{2,1,0:T(8,128)S(1)} custom-call(f32[4,8,2304]{2,1,0:T(8,128)S(1)} %copy-done.3, f32[3,3,36,108]{3,2,1,0:T(8,128)S(1)} %copy-done.5, f32[3,3,36,108]{3,2,1,0:T(8,128)S(1)} %copy-done.6, f32[1,2,36,432]{3,2,1,0:T(8,128)S(1)} %copy.15.sr_hbm, f32[1,2,36,432]{3,2,1,0:T(8,128)S(1)} %copy.16.si_hbm, ...), custom_call_target="tpu_custom_call" | custom-call | tf_op jit(solution)/shard_map/pallas_call | solution.py:530
  84.6 1.3 %fusion.1 = f32[4,8,2304]{2,1,0:T(8,128)} fusion(f32[4,8,2304]{2,1,0:T(8,128)S(1)} %shard_map.136), kind=kLoop, calls=%fused_computation.2 | loop fusion | flops 4718592 | bytes 589824 | tf_op jit(solution)/shard_map/mul | solution.py:540
Async XLA Ops:
  1.9 1.3 %copy-start = (bf16[2,2,256,640]{3,2,1,0:T(8,128)(2,1)S(1)}, bf16[2,2,256,640]{3,2,1,0:T(8,128)(2,1)}, u32[]{:S(2)}) copy-start(bf16[2,2,256,640]{3,2,1,0:T(8,128)(2,1)} %constant.86.clone.fi_hbm) | copy-start | bytes 3932164
  3.2 1.1 %copy-start.1 = (bf16[2,704,256]{2,1,0:T(8,128)(2,1)S(1)}, bf16[2,704,256]{2,1,0:T(8,128)(2,1)}, u32[]{:S(2)}) copy-start(bf16[2,704,256]{2,1,0:T(8,128)(2,1)} %constant.78.clone.fz_hbm) | copy-start | bytes 2162692
  4.3 1.0 %copy-start.2 = (bf16[512,512]{1,0:T(8,128)(2,1)S(1)}, bf16[512,512]{1,0:T(8,128)(2,1)}, u32[]{:S(2)}) copy-start(bf16[512,512]{1,0:T(8,128)(2,1)} %constant.85.clone.pm_hbm) | copy-start | bytes 1572868
  5.4 1.0 %copy-start.3 = (f32[4,8,2304]{2,1,0:T(8,128)S(1)}, f32[4,8,2304]{2,1,0:T(8,128)}, u32[]{:S(2)}) copy-start(f32[4,8,2304]{2,1,0:T(8,128)} %state_hbm.1) | copy-start | bytes 884740
  6.3 0.9 %copy-start.4 = (bf16[16,64,32]{2,1,0:T(8,128)(2,1)S(1)}, bf16[16,64,32]{2,1,0:T(8,128)(2,1)}, u32[]{:S(2)}) copy-start(bf16[16,64,32]{2,1,0:T(8,128)(2,1)} %constant.80.clone.d2_hbm) | copy-start | bytes 196612
  7.3 0.9 %copy-start.5 = (f32[3,3,36,108]{3,2,1,0:T(8,128)S(1)}, f32[3,3,36,108]{3,2,1,0:T(8,128)}, u32[]{:S(2)}) copy-start(f32[3,3,36,108]{3,2,1,0:T(8,128)} %wf_hbm.1) | copy-start | bytes 419908
  8.2 0.9 %copy-start.6 = (f32[3,3,36,108]{3,2,1,0:T(8,128)S(1)}, f32[3,3,36,108]{3,2,1,0:T(8,128)}, u32[]{:S(2)}) copy-start(f32[3,3,36,108]{3,2,1,0:T(8,128)} %ws_hbm.1) | copy-start | bytes 419908
  9.1 0.9 %copy-start.7 = (bf16[128,512]{1,0:T(8,128)(2,1)S(1)}, bf16[128,512]{1,0:T(8,128)(2,1)}, u32[]{:S(2)}) copy-start(bf16[128,512]{1,0:T(8,128)(2,1)} %constant.84.clone.ex_hbm) | copy-start | bytes 393220
  10.0 0.9 %copy-start.8 = (f32[4,40,128]{2,1,0:T(8,128)S(1)}, f32[4,40,128]{2,1,0:T(8,128)}, u32[]{:S(2)}) copy-start(f32[4,40,128]{2,1,0:T(8,128)} %constant.83.clone.mk_hbm) | copy-start | bytes 245764
  10.9 0.8 copy-start.9
  11.8 0.8 copy-start.10
  12.6 0.8 copy-start.11

commit v2 on v1

--- a/solution.py
+++ b/solution.py
@@ -28,12 +28,9 @@
     return high, low
 
 
-def stacked(table, pad=0):
+def stacked(table):
     high, low = halves(table)
-    parts = [high, high, low]
-    if pad:
-        parts.append(np.zeros(high.shape[:-1] + (pad,), high.dtype))
-    return np.concatenate(parts, axis=-1)
+    return np.concatenate([high, high, low], axis=-1)
 
 
 def tables():
@@ -57,11 +54,14 @@
         angle = 2 * np.pi * (np.outer(first, second) % 128) / 128
         return np.concatenate([np.cos(angle), np.sin(angle)], axis=0)
 
-    xs = [np.arange(32) + 32 * g for g in range(4)]
-    ys = [np.arange(NY) + NY * g for g in range(GY)]
+    members = np.array([[(t // 2) * 8 + g * 2 + t % 2 for t in range(GROUP)] for g in range(4)])
+    xs = [(members[g][:, None] * NX + np.arange(NX)[None, :]).reshape(32) for g in range(4)]
+    blocks = np.arange(4) * 4
+    ys = [((blocks[:, None] + g) * NY + np.arange(NY)[None, :]).reshape(32) for g in range(4)]
+    halved = np.concatenate([freq[0::2], freq[1::2]])
     d1 = stacked(np.stack([pair(freq, v) for v in xs]))
-    d2 = stacked(np.stack([pair(freq, v) for v in ys]), 8)
-    d4 = stacked(np.stack([pair(v, freq) for v in ys]))
+    d2 = stacked(np.stack([pair(halved, v) for v in ys]))
+    d4 = stacked(np.stack([pair(v, halved) for v in ys]))
     d5 = stacked(np.stack([pair(v, freq) for v in xs]))
     mask = np.zeros((4, 40, 128), np.float32)
     spread = np.zeros((128, 512))
@@ -117,19 +117,24 @@
 ):
     i = lax.axis_index("gx")
     j = lax.axis_index("gy")
-    a = i // GROUP
-    l = i % GROUP
+    g = (i % 8) // 2
+    l = (i // 8) * 2 + i % 2
+    yy = j // 4
+    zz = j % 4
 
     sources = [
-        (state_hbm, st), (fz_hbm, fz), (d1_hbm.at[a], d1), (d2_hbm.at[j], d2), (wf_hbm, wf),
-        (ws_hbm, ws), (sr_hbm.at[0], sr), (si_hbm.at[0], si), (mk_hbm, mk), (ex_hbm, ex),
-        (pm_hbm, pm), (d4_hbm.at[j], d4), (d5_hbm.at[a], d5), (fi_hbm, fi),
+        (state_hbm, st), (fz_hbm, fz), (d1_hbm.at[g], d1), (d2_hbm.at[zz], d2), (wf_hbm, wf),
+        (ws_hbm, ws), (sr_hbm, sr), (si_hbm, si), (mk_hbm, mk), (ex_hbm, ex),
+        (pm_hbm, pm), (d4_hbm.at[zz], d4), (d5_hbm.at[g], d5), (fi_hbm, fi),
     ]
     loads = [pltpu.make_async_copy(src, dst, load_sem.at[n]) for n, (src, dst) in enumerate(sources)]
-    for load in loads:
-        load.start()
+    loads[0].start()
+    loads[1].start()
     (l_st, l_fz, l_d1, l_d2, l_wf, l_ws, l_sr, l_si, l_mk, l_ex, l_pm, l_d4, l_d5, l_fi) = loads
 
+    def peer(t, y):
+        return ((t // 2) * 8 + g * 2 + t % 2, y * 4 + zz)
+
     barrier = pltpu.get_barrier_semaphore()
 
     @pl.loop(1, GX)
@@ -139,6 +144,14 @@
     @pl.loop(1, GY)
     def _(s):
         pl.semaphore_signal(barrier, inc=1, device_id=(i, (j + s) % GY), device_id_type=MESH)
+
+    @pl.loop(1, GROUP)
+    def _(s):
+        for n in range(1, 4):
+            pl.semaphore_signal(
+                barrier, inc=1, device_id=peer((l + s) % GROUP, (yy + n) % 4), device_id_type=MESH
+            )
+
 
     def remote(src, dst, stage_no, device):
         return pltpu.make_async_remote_copy(
@@ -160,12 +173,7 @@
     lane = lax.broadcasted_iota(jnp.int32, (1, 128), 1)
     first_half = lane < 64
 
-    cc[...] = jnp.zeros_like(cc)
     l_st.wait()
-    t2 = tt.reshape(8 * 12 * 24, 128)
-    for x in range(NX):
-        for m in range(18):
-            t2[pl.ds(((x + 2) * 12 + 2) * 24 + m, 8, stride=24), :] = st[x, :, m * 128 : (m + 1) * 128]
     l_fz.wait()
     field = st[...].reshape(NX * NY, C * Z)
     for e in range(2):
@@ -177,17 +185,26 @@
         for h in range(2):
             for part in range(2):
                 for x in range(NX):
-                    s1[pl.ds(x * 8 + part * 4 + 2 * h + e, 8, stride=32), :] = res[
+                    s1[pl.ds((2 * h + e) * 64 + x * 2 + part, 8, stride=8), :] = res[
                         h * 32 + x * 8 : h * 32 + x * 8 + 8, part * 128 : part * 128 + 128
                     ]
-    pl.semaphore_wait(barrier, GX - 1 + GY - 1)
-
-    @pl.loop(1, GROUP)
-    def _(s):
-        t = (l + s) % GROUP
-        remote(s1.at[rows(t * 32, 32)], r1.at[rows(l * 32, 32)], 0, (a * GROUP + t, j)).start()
-
-    r1[rows(l * 32, 32), :] = s1[rows(l * 32, 32), :]
+    pl.semaphore_wait(barrier, GX - 1 + GY - 1 + 21)
+    slot = yy * 8 + l
+
+    @pl.loop(1, 32)
+    def _(s):
+        n = (slot + s) % 32
+        remote(s1.at[rows(n * 8, 8)], r1.at[rows(slot * 8, 8)], 0, peer(n % 8, n // 8)).start()
+
+    r1[rows(slot * 8, 8), :] = s1[rows(slot * 8, 8), :]
+    for load in loads[2:]:
+        load.start()
+
+    cc[...] = jnp.zeros_like(cc)
+    t2 = tt.reshape(8 * 12 * 24, 128)
+    for x in range(NX):
+        for m in range(18):
+            t2[pl.ds(((x + 2) * 12 + 2) * 24 + m, 8, stride=24), :] = st[x, :, m * 128 : (m + 1) * 128]
 
     def halo(n, src, dst, device):
         return pltpu.make_async_remote_copy(
@@ -199,14 +216,6 @@
     up_y = halo(1, tt.at[2:6, 8:10], tt.at[2:6, 0:2], (i, (j + 1) % GY))
     down_x = halo(2, tt.at[2:4], tt.at[6:8], ((i + GX - 1) % GX, j))
     up_x = halo(3, tt.at[4:6], tt.at[0:2], ((i + 1) % GX, j))
-
-    @pl.when(j > 0)
-    def _():
-        down_y.start()
-
-    @pl.when(j < GY - 1)
-    def _():
-        up_y.start()
 
     @pl.when(j == 0)
     def _():
@@ -233,10 +242,18 @@
                 scratch[0:36, tap * KB : tap * KB + 108] = high
                 scratch[40:76, tap * KB : tap * KB + 108] = low
 
+    @pl.when(j > 0)
+    def _():
+        down_y.start()
+
+    @pl.when(j < GY - 1)
+    def _():
+        up_y.start()
+
     l_wf.wait()
     filters(wf, wst1)
 
-    wait_recv(r1, 7 * 32, 0)
+    wait_recv(r1, 31 * 8, 0)
     l_d1.wait()
 
     def gathered(buffer):
@@ -246,49 +263,53 @@
         high, low = split(value)
         return jnp.concatenate([high, low, high], axis=0)
 
-    def combine(res, count, sign):
-        top, bottom = res[:count], res[count:]
-        real = top[:, :512] + sign * bottom[:, 512:]
-        imag = top[:, 512:] - sign * bottom[:, :512]
+    def exchanged(buffer):
+        return jnp.concatenate(
+            [buffer[pl.ds(y * 64 + part, 32, stride=2), :] for part in range(2) for y in range(4)], axis=1
+        )
+
+    def combine(res, sign):
+        half = res.shape[1] // 2
+        top, bottom = res[:32], res[32:]
+        real = top[:, :half] + sign * bottom[:, half:]
+        imag = top[:, half:] - sign * bottom[:, :half]
         return real, imag
 
-    def scatter_rows(buffer, real, imag, count):
-        for k in range(4):
-            buffer[pl.ds(k, count, stride=8), :] = real[:, k * 128 : k * 128 + 128]
-            buffer[pl.ds(k + 4, count, stride=8), :] = imag[:, k * 128 : k * 128 + 128]
-
-    res = dot(d1[...], tripled(gathered(r1)))
-    real, imag = combine(res, 32, 1.0)
-    scatter_rows(s2, real, imag, 32)
+    real, imag = combine(dot(d1[...], tripled(exchanged(r1))), 1.0)
+    for k in range(4):
+        s2[pl.ds(k, 32, stride=8), :] = real[:, k * 128 : k * 128 + 128]
+        s2[pl.ds(k + 4, 32, stride=8), :] = imag[:, k * 128 : k * 128 + 128]
 
     @pl.loop(1, GX)
     def _(s):
         t = (i + s) % GX
-        remote(s2.at[rows(t * 8, 8)], r2.at[rows(i * 8, 8)], 1, (t, j)).start()
-
-    r2[rows(i * 8, 8), :] = s2[rows(i * 8, 8), :]
+        remote(s2.at[rows(t * 8, 8)], r2.at[rows((g * 8 + l) * 8, 8)], 1, (t, j)).start()
+
+    r2[rows((g * 8 + l) * 8, 8), :] = s2[rows(i * 8, 8), :]
     l_ws.wait()
     filters(ws, wst2)
 
     wait_recv(r2, 31 * 8, 1)
     l_d2.wait()
-    summed = []
-    for k in range(8):
-        total = r2[pl.ds(k, 8, stride=8), :]
-        for g in range(1, 4):
-            total = total + r2[pl.ds(g * 64 + k, 8, stride=8), :]
-        summed.append(total)
-    high, low = split32(jnp.concatenate(summed, axis=1))
-    right = jnp.concatenate([high, low, high, jnp.zeros_like(high)], axis=0).astype(BF16)
-    real, imag = combine(dot(d2[...], right), 32, 1.0)
-    scatter_rows(s3, real, imag, 32)
+    parts = []
+    for part in range(2):
+        column = []
+        for y in range(4):
+            k = part * 4 + y
+            terms = [r2[pl.ds(n * 64 + k, 8, stride=8), :] for n in range(4)]
+            column.append((terms[0] + terms[1]) + (terms[2] + terms[3]))
+        parts.append(jnp.concatenate(column, axis=0))
+    result = combine(dot(d2[...], tripled(jnp.concatenate(parts, axis=1))), 1.0)
+    for b in range(2):
+        for part in range(2):
+            s3[:, b * 2 + part, :] = result[part][b * 16 : b * 16 + 16]
 
     @pl.loop(1, GY)
     def _(s):
         t = (j + s) % GY
-        remote(s3.at[rows(t * 16, 16)], r3.at[rows(j * 16, 16)], 2, (i, t)).start()
-
-    r3[rows(j * 16, 16), :] = s3[rows(j * 16, 16), :]
+        remote(s3.at[t], r3.at[j], 2, (i, t)).start()
+
+    r3[j] = s3[j]
 
     @pl.when(j > 0)
     def _():
@@ -306,19 +327,17 @@
     def _():
         up_x.start()
 
-    wait_recv(r3, 15 * 16, 2)
-    total = r3[0:16, :]
-    for n in range(1, GY):
-        total = total + r3[n * 16 : n * 16 + 16, :]
+    wait_recv(r3, GY - 1, 2)
+    total = [(r3[4 * n] + r3[4 * n + 1]) + (r3[4 * n + 2] + r3[4 * n + 3]) for n in range(4)]
     for load in (l_mk, l_ex, l_sr, l_si, l_pm):
         load.wait()
     placed = []
     for q in range(2):
         for part in range(2):
             acc = None
-            for g in range(4):
-                n = q * 8 + part * 4 + g
-                term = total[n : n + 1, :] * mk[g]
+            for cg in range(4):
+                n = q * 2 + part
+                term = total[cg][n : n + 1, :] * mk[cg]
                 acc = term if acc is None else acc + term
             placed.append(acc)
     high, low = split(jnp.concatenate(placed, axis=0))
@@ -327,20 +346,21 @@
     for q in range(2):
         c_re = wide[q * 80 : q * 80 + 36, :432]
         c_im = wide[q * 80 + 40 : q * 80 + 76, :432]
-        m8[2 * q : 2 * q + 1, 0:432] = jnp.sum(c_re * sr[q] - c_im * si[q], axis=0, keepdims=True)
-        m8[2 * q + 1 : 2 * q + 2, 0:432] = jnp.sum(c_re * si[q] + c_im * sr[q], axis=0, keepdims=True)
+        w_re, w_im = sr[:, q, :], si[:, q, :]
+        m8[2 * q : 2 * q + 1, 0:432] = jnp.sum(c_re * w_re - c_im * w_im, axis=0, keepdims=True)
+        m8[2 * q + 1 : 2 * q + 2, 0:432] = jnp.sum(c_re * w_im + c_im * w_re, axis=0, keepdims=True)
     high, low = split32(m8[...])
     moved = dot(jnp.concatenate([high, low], axis=0).astype(BF16), pm[...])
     mixed = moved[0:8] + moved[8:16]
-    for g in range(4):
-        s4[pl.ds(g, 4, stride=4), :] = mixed[0:4, g * 128 : g * 128 + 128]
+    for cg in range(4):
+        s4[cg] = mixed[0:4, cg * 128 : cg * 128 + 128]
 
     @pl.loop(1, GY)
     def _(s):
         t = (j + s) % GY
-        remote(s4, r4.at[rows(j * 16, 16)], 3, (i, t)).start()
-
-    r4[rows(j * 16, 16), :] = s4[...]
+        remote(s4.at[t // 4], r4.at[j], 3, (i, t)).start()
+
+    r4[j] = s4[yy]
 
     @pl.when(i > 0)
     def _():
@@ -399,15 +419,21 @@
         keep = keep_y * jnp.where(outside, 0.0, 1.0)
         hid[rows(x * 40, 40), :] = gelu(value) * keep
 
-    wait_recv(r4, 15 * 16, 3)
+    wait_recv(r4, GY - 1, 3)
     l_d4.wait()
-    real, imag = combine(dot(d4[...], tripled(gathered(r4))), 8, -1.0)
-    scatter_rows(s5, real, imag, 8)
+    modes = jnp.concatenate(
+        [jnp.concatenate([r4[:, b * 2 + part, :] for b in range(2)], axis=0) for part in range(2)], axis=1
+    )
+    result = combine(dot(d4[...], tripled(modes)), -1.0)
+    for part in range(2):
+        for y in range(4):
+            s5[pl.ds(part * 4 + y, 8, stride=8), :] = result[part][y * 8 : y * 8 + 8]
 
     @pl.loop(1, GX)
     def _(s):
         t = (i + s) % GX
-        remote(s5.at[rows((t % GROUP) * 8, 8)], r5.at[rows(i * 8, 8)], 4, (t, j)).start()
+        row = (t // 8) * 2 + t % 2
+        remote(s5.at[rows(row * 8, 8)], r5.at[rows(i * 8, 8)], 4, (t, j)).start()
 
     r5[rows(i * 8, 8), :] = s5[rows(l * 8, 8), :]
 
@@ -427,15 +453,17 @@
 
     wait_recv(r5, 31 * 8, 4)
     l_d5.wait()
-    real, imag = combine(dot(d5[...], tripled(gathered(r5))), 32, -1.0)
-    scatter_rows(s6, real, imag, 32)
-
-    @pl.loop(1, GROUP)
-    def _(s):
-        t = (l + s) % GROUP
-        remote(s6.at[rows(t * 32, 32)], r6.at[rows(l * 32, 32)], 5, (a * GROUP + t, j)).start()
-
-    r6[rows(l * 32, 32), :] = s6[rows(l * 32, 32), :]
+    result = combine(dot(d5[...], tripled(gathered(r5))), -1.0)
+    for part in range(2):
+        for y in range(4):
+            s6[pl.ds(y * 64 + part, 32, stride=2), :] = result[part][:, y * 128 : y * 128 + 128]
+
+    @pl.loop(1, 32)
+    def _(s):
+        n = (slot + s) % 32
+        remote(s6.at[rows(n * 8, 8)], r6.at[rows(slot * 8, 8)], 5, peer(n % 8, n // 8)).start()
+
+    r6[rows(slot * 8, 8), :] = s6[rows(slot * 8, 8), :]
 
     w2 = wst2[...].astype(BF16)
 
@@ -457,7 +485,7 @@
         for m in range(18):
             co[rows(x * 8, 8), m * 128 : m * 128 + 128] = n2[pl.ds(m, 8, stride=24), :]
 
-    wait_recv(r6, 7 * 32, 5)
+    wait_recv(r6, 31 * 8, 5)
     l_fi.wait()
     results = []
     for e in range(2):
@@ -466,7 +494,7 @@
                 jnp.concatenate(
                     [
                         jnp.concatenate(
-                            [r6[pl.ds(x * 8 + part * 4 + 2 * h + e, 8, stride=32), :] for x in range(NX)], axis=0
+                            [r6[pl.ds((2 * h + e) * 64 + x * 2 + part, 8, stride=8), :] for x in range(NX)], axis=0
                         )
                         for part in range(2)
                     ],
@@ -485,12 +513,12 @@
         for x in range(NX):
             out_ref[x, :, h * 1152 : h * 1152 + 1152] = full[x * 8 : x * 8 + 8]
 
-    wait_send(s1, 7 * 32, 0)
+    wait_send(s1, 31 * 8, 0)
     wait_send(s2, 31 * 8, 1)
-    wait_send(s3, 15 * 16, 2)
-    wait_send(r4, 15 * 16, 3)
+    wait_send(r3, GY - 1, 2)
+    wait_send(r4, GY - 1, 3)
     wait_send(r5, 31 * 8, 4)
-    wait_send(s6, 7 * 32, 5)
+    wait_send(s6, 31 * 8, 5)
 
     @pl.when(j > 0)
     def _():
@@ -514,11 +542,11 @@
     vm = pltpu.VMEM
     scratch = [
         vm((NX, NY, C * Z), F32), vm((3, 3, C, 3 * C), F32), vm((3, 3, C, 3 * C), F32),
-        vm((2, C, MZ * C), F32), vm((2, C, MZ * C), F32),
-        vm((2, 704, 256), BF16), vm((64, 96), BF16), vm((64, 32), BF16), vm((16, 96), BF16), vm((64, 96), BF16),
+        vm((C, 2, MZ * C), F32), vm((C, 2, MZ * C), F32),
+        vm((2, 704, 256), BF16), vm((64, 96), BF16), vm((64, 96), BF16), vm((64, 96), BF16), vm((64, 96), BF16),
         vm((4, 40, 128), F32), vm((128, 512), BF16), vm((512, 512), BF16), vm((2, 2, 256, 640), BF16),
         vm((256, 128), F32), vm((256, 128), F32), vm((256, 128), F32), vm((256, 128), F32),
-        vm((256, 128), F32), vm((256, 128), F32), vm((16, 128), F32), vm((256, 128), F32),
+        vm((GY, 4, 128), F32), vm((GY, 4, 128), F32), vm((4, 4, 128), F32), vm((GY, 4, 128), F32),
         vm((64, 128), F32), vm((256, 128), F32), vm((256, 128), F32), vm((256, 128), F32),
         vm((8, 12, 24, 128), F32), vm((8, 512), F32), vm((80, 9 * KB), F32), vm((80, 9 * KB), F32),
         vm((280, 128), F32), vm((7 * KB, 128), F32), vm((8 * 336, 640), BF16), vm((8 * 336, 640), BF16),
@@ -534,9 +562,12 @@
         out_specs=pl.BlockSpec(memory_space=pltpu.VMEM),
         scratch_shapes=scratch,
         compiler_params=pltpu.CompilerParams(
-            collective_id=0, has_side_effects=True, vmem_limit_bytes=40 * 1024 * 1024
+            collective_id=0, has_side_effects=True, vmem_limit_bytes=56 * 1024 * 1024
         ),
-    )(state_field, conv_first, conv_second, spec_real, spec_imag, *constants)
+    )(
+        state_field, conv_first, conv_second,
+        jnp.transpose(spec_real[0], (1, 0, 2)), jnp.transpose(spec_imag[0], (1, 0, 2)), *constants
+    )
     return jax.nn.gelu(before, approximate=False)
 
 

time: 86.5 us -> 65.6 us (0.76)
  local copies, waits for them, and re-layouts: 13.4 us -> 0 us
  Pallas kernels: 71.1 us -> 63.1 us
  other arithmetic: 1.35 us -> 2.31 us
    unnamed x26 -> x0, local copies, waits for them, and re-layouts: 13.4 us -> none
    pallas_call x1, Pallas kernels: 71.1 us -> 63.1 us  [on_device(): pl.pallas_call(kernel, out_shape=jax.ShapeDtypeStruct((NX, NY, C * Z), F3...]
    mul x1, other arithmetic: 1.35 us -> 2.31 us  [on_device(): return jax.nn.gelu(before, approximate=False)]
where the time goes in v2:
time: 65.6 us; the launch traced here: 65.5 us
  Pallas kernels  63.1 us (96%)
  other arithmetic  2.31 us (4%)
    pallas_call x1, Pallas kernels, on_device(): pl.pallas_call(kernel, out_shape=jax.ShapeDtypeStruct((NX, NY, C * Z), F3...  63.1 us
    mul x1, other arithmetic, on_device(): return jax.nn.gelu(before, approximate=False)  2.31 us

profile of v2, /device:TPU:1, one launch (start us, length us, event | category | flops | bytes accessed | tf_op | source)
XLA Modules:
  0.0 65.5 jit_solution(13635976297218446328)
XLA Ops:
  0.0 63.1 %shard_map.136 = f32[4,8,2304]{2,1,0:T(8,128)} custom-call(f32[4,8,2304]{2,1,0:T(8,128)} %state_hbm.1, f32[3,3,36,108]{3,2,1,0:T(8,128)} %wf_hbm.1, f32[3,3,36,108]{3,2,1,0:T(8,128)} %ws_hbm.1, f32[36,2,432]{2,1,0:T(2,128)} %bitcast.6, f32[36,2,432]{2,1,0:T(2,128)} %bitcast.7, bf16[2,704,256]{2,1,0:T(8,128)(2,1)} %constant.78.clone.fz_hbm, ...), custom_call_target="tpu_custom_call" | custom-call | tf_op jit(solution)/shard_map/pallas_call | solution.py:558
  63.1 2.3 %fusion.1 = f32[4,8,2304]{2,1,0:T(8,128)} fusion(f32[4,8,2304]{2,1,0:T(8,128)} %shard_map.136), kind=kLoop, calls=%fused_computation.2 | loop fusion | flops 4718592 | bytes 589824 | tf_op jit(solution)/shard_map/mul | solution.py:571

commit v3 on v2

--- a/solution.py
+++ b/solution.py
@@ -113,7 +113,7 @@
     st, wf, ws, sr, si, fz, d1, d2, d4, d5, mk, ex, pm, fi,
     s1, r1, s2, r2, s3, r3, s4, r4, s5, r5, s6, r6,
     tt, m8, wst1, wst2, cc, stage, ubh, ubl, hid, stage2, ub2h, ub2l, ct, n2, co,
-    load_sem, send_sem, recv_sem, halo_send, halo_recv,
+    load_sem, send_sem, recv_sem, halo_send, halo_recv, ready_sem,
 ):
     i = lax.axis_index("gx")
     j = lax.axis_index("gy")
@@ -137,13 +137,20 @@
 
     barrier = pltpu.get_barrier_semaphore()
 
-    @pl.loop(1, GX)
-    def _(s):
-        pl.semaphore_signal(barrier, inc=1, device_id=((i + s) % GX, j), device_id_type=MESH)
-
-    @pl.loop(1, GY)
-    def _(s):
-        pl.semaphore_signal(barrier, inc=1, device_id=(i, (j + s) % GY), device_id_type=MESH)
+    across = [(i, yy * 4 + (zz + 1) % 4), (i, yy * 4 + (zz + 3) % 4)]
+    for device in across:
+        pl.semaphore_signal(barrier, inc=1, device_id=device, device_id_type=MESH)
+
+    above = (zz == 3) & (j < GY - 1)
+    below = (zz == 0) & (j > 0)
+
+    @pl.when(above)
+    def _():
+        pl.semaphore_signal(barrier, inc=1, device_id=(i, (j + 1) % GY), device_id_type=MESH)
+
+    @pl.when(below)
+    def _():
+        pl.semaphore_signal(barrier, inc=1, device_id=(i, (j + GY - 1) % GY), device_id_type=MESH)
 
     @pl.loop(1, GROUP)
     def _(s):
@@ -152,6 +159,13 @@
                 barrier, inc=1, device_id=peer((l + s) % GROUP, (yy + n) % 4), device_id_type=MESH
             )
 
+    for n in range(1, 4):
+        pl.semaphore_signal(barrier, inc=1, device_id=peer(l, (yy + n) % 4), device_id_type=MESH)
+
+
+    @pl.loop(1, GX)
+    def _(s):
+        pl.semaphore_signal(barrier, inc=1, device_id=((i + s) % GX, j), device_id_type=MESH)
 
     def remote(src, dst, stage_no, device):
         return pltpu.make_async_remote_copy(
@@ -188,7 +202,8 @@
                     s1[pl.ds((2 * h + e) * 64 + x * 2 + part, 8, stride=8), :] = res[
                         h * 32 + x * 8 : h * 32 + x * 8 + 8, part * 128 : part * 128 + 128
                     ]
-    pl.semaphore_wait(barrier, GX - 1 + GY - 1 + 21)
+    near = GX - 1 + 24 + 2
+    pl.semaphore_wait(barrier, jnp.where(above | below, near + 1, near))
     slot = yy * 8 + l
 
     @pl.loop(1, 32)
@@ -254,6 +269,8 @@
     filters(wf, wst1)
 
     wait_recv(r1, 31 * 8, 0)
+    for device in across:
+        pl.semaphore_signal(ready_sem, inc=1, device_id=device, device_id_type=MESH)
     l_d1.wait()
 
     def gathered(buffer):
@@ -303,6 +320,8 @@
     for b in range(2):
         for part in range(2):
             s3[:, b * 2 + part, :] = result[part][b * 16 : b * 16 + 16]
+
+    pl.semaphore_wait(ready_sem, 2)
 
     @pl.loop(1, GY)
     def _(s):
@@ -553,7 +572,7 @@
         vm((240, 640), F32), vm((8 * KB, 128), F32), vm((6 * 336, 512), BF16), vm((6 * 336, 512), BF16),
         vm((160, 128), F32), vm((192, 128), F32), vm((32, C * Z), F32),
         pltpu.SemaphoreType.DMA((14,)), pltpu.SemaphoreType.DMA((6,)), pltpu.SemaphoreType.DMA((6,)),
-        pltpu.SemaphoreType.DMA((4,)), pltpu.SemaphoreType.DMA((4,)),
+        pltpu.SemaphoreType.DMA((4,)), pltpu.SemaphoreType.DMA((4,)), pltpu.SemaphoreType.REGULAR,
     ]
     before = pl.pallas_call(
         kernel,

time: 65.6 us -> 62.4 us (0.951)
  Pallas kernels: 63.1 us -> 59.9 us
    pallas_call x1, Pallas kernels: 63.1 us -> 59.9 us  [on_device(): pl.pallas_call(kernel, out_shape=jax.ShapeDtypeStruct((NX, NY, C * Z), F3...]
where the time goes in v3:
time: 62.4 us; the launch traced here: 62.2 us
  Pallas kernels  59.9 us (96%)
  other arithmetic  2.31 us (4%)
    pallas_call x1, Pallas kernels, on_device(): pl.pallas_call(kernel, out_shape=jax.ShapeDtypeStruct((NX, NY, C * Z), F3...  59.9 us
    mul x1, other arithmetic, on_device(): return jax.nn.gelu(before, approximate=False)  2.31 us

profile of v3, /device:TPU:1, one launch (start us, length us, event | category | flops | bytes accessed | tf_op | source)
XLA Modules:
  0.0 62.2 jit_solution(2960999031959743303)
XLA Ops:
  0.0 59.9 %shard_map.136 = f32[4,8,2304]{2,1,0:T(8,128)} custom-call(f32[4,8,2304]{2,1,0:T(8,128)} %state_hbm.1, f32[3,3,36,108]{3,2,1,0:T(8,128)} %wf_hbm.1, f32[3,3,36,108]{3,2,1,0:T(8,128)} %ws_hbm.1, f32[36,2,432]{2,1,0:T(2,128)} %bitcast.6, f32[36,2,432]{2,1,0:T(2,128)} %bitcast.7, bf16[2,704,256]{2,1,0:T(8,128)(2,1)} %constant.78.clone.fz_hbm, ...), custom_call_target="tpu_custom_call" | custom-call | tf_op jit(solution)/shard_map/pallas_call | solution.py:577
  59.9 2.3 %fusion.1 = f32[4,8,2304]{2,1,0:T(8,128)} fusion(f32[4,8,2304]{2,1,0:T(8,128)} %shard_map.136), kind=kLoop, calls=%fused_computation.2 | loop fusion | flops 4718592 | bytes 589824 | tf_op jit(solution)/shard_map/mul | solution.py:590

commit v4 on v3

--- a/solution.py
+++ b/solution.py
@@ -152,9 +152,13 @@
     def _():
         pl.semaphore_signal(barrier, inc=1, device_id=(i, (j + GY - 1) % GY), device_id_type=MESH)
 
+    for n in range(1, 4):
+        along = (i // 8) * 8 + ((g + n) % 4) * 2 + i % 2
+        pl.semaphore_signal(barrier, inc=1, device_id=(along, j), device_id_type=MESH)
+
     @pl.loop(1, GROUP)
     def _(s):
-        for n in range(1, 4):
+        for n in range(4):
             pl.semaphore_signal(
                 barrier, inc=1, device_id=peer((l + s) % GROUP, (yy + n) % 4), device_id_type=MESH
             )
@@ -162,10 +166,6 @@
     for n in range(1, 4):
         pl.semaphore_signal(barrier, inc=1, device_id=peer(l, (yy + n) % 4), device_id_type=MESH)
 
-
-    @pl.loop(1, GX)
-    def _(s):
-        pl.semaphore_signal(barrier, inc=1, device_id=((i + s) % GX, j), device_id_type=MESH)
 
     def remote(src, dst, stage_no, device):
         return pltpu.make_async_remote_copy(
@@ -202,25 +202,14 @@
                     s1[pl.ds((2 * h + e) * 64 + x * 2 + part, 8, stride=8), :] = res[
                         h * 32 + x * 8 : h * 32 + x * 8 + 8, part * 128 : part * 128 + 128
                     ]
-    near = GX - 1 + 24 + 2
-    pl.semaphore_wait(barrier, jnp.where(above | below, near + 1, near))
-    slot = yy * 8 + l
-
-    @pl.loop(1, 32)
-    def _(s):
-        n = (slot + s) % 32
-        remote(s1.at[rows(n * 8, 8)], r1.at[rows(slot * 8, 8)], 0, peer(n % 8, n // 8)).start()
-
-    r1[rows(slot * 8, 8), :] = s1[rows(slot * 8, 8), :]
-    for load in loads[2:]:
-        load.start()
-
     cc[...] = jnp.zeros_like(cc)
     t2 = tt.reshape(8 * 12 * 24, 128)
     for x in range(NX):
         for m in range(18):
             t2[pl.ds(((x + 2) * 12 + 2) * 24 + m, 8, stride=24), :] = st[x, :, m * 128 : (m + 1) * 128]
 
+    near = 31 + 3 + 2
+    pl.semaphore_wait(barrier, jnp.where(above | below, near + 1, near))
     def halo(n, src, dst, device):
         return pltpu.make_async_remote_copy(
             src_ref=src, dst_ref=dst, send_sem=halo_send.at[n], recv_sem=halo_recv.at[n],
@@ -231,6 +220,25 @@
     up_y = halo(1, tt.at[2:6, 8:10], tt.at[2:6, 0:2], (i, (j + 1) % GY))
     down_x = halo(2, tt.at[2:4], tt.at[6:8], ((i + GX - 1) % GX, j))
     up_x = halo(3, tt.at[4:6], tt.at[0:2], ((i + 1) % GX, j))
+
+    @pl.when(j > 0)
+    def _():
+        down_y.start()
+
+    @pl.when(j < GY - 1)
+    def _():
+        up_y.start()
+
+    slot = yy * 8 + l
+
+    @pl.loop(1, 32)
+    def _(s):
+        n = (slot + s) % 32
+        remote(s1.at[rows(n * 8, 8)], r1.at[rows(slot * 8, 8)], 0, peer(n % 8, n // 8)).start()
+
+    r1[rows(slot * 8, 8), :] = s1[rows(slot * 8, 8), :]
+    for load in loads[2:]:
+        load.start()
 
     @pl.when(j == 0)
     def _():
@@ -256,14 +264,6 @@
                 high, low = split32(src[tap_x, tap_y])
                 scratch[0:36, tap * KB : tap * KB + 108] = high
                 scratch[40:76, tap * KB : tap * KB + 108] = low
-
-    @pl.when(j > 0)
-    def _():
-        down_y.start()
-
-    @pl.when(j < GY - 1)
-    def _():
-        up_y.start()
 
     l_wf.wait()
     filters(wf, wst1)

time: 62.4 us -> 61.9 us (level)
  no operation moved by 1% of the time
where the time goes in v4:
time: 61.9 us; the launch traced here: 61.7 us
  Pallas kernels  59.4 us (96%)
  other arithmetic  2.31 us (4%)
    pallas_call x1, Pallas kernels, on_device(): pl.pallas_call(kernel, out_shape=jax.ShapeDtypeStruct((NX, NY, C * Z), F3...  59.4 us
    mul x1, other arithmetic, on_device(): return jax.nn.gelu(before, approximate=False)  2.31 us

profile of v4, /device:TPU:1, one launch (start us, length us, event | category | flops | bytes accessed | tf_op | source)
XLA Modules:
  0.0 61.7 jit_solution(12620515948768291321)
XLA Ops:
  0.0 59.4 %shard_map.136 = f32[4,8,2304]{2,1,0:T(8,128)} custom-call(f32[4,8,2304]{2,1,0:T(8,128)} %state_hbm.1, f32[3,3,36,108]{3,2,1,0:T(8,128)} %wf_hbm.1, f32[3,3,36,108]{3,2,1,0:T(8,128)} %ws_hbm.1, f32[36,2,432]{2,1,0:T(2,128)} %bitcast.6, f32[36,2,432]{2,1,0:T(2,128)} %bitcast.7, bf16[2,704,256]{2,1,0:T(8,128)(2,1)} %constant.78.clone.fz_hbm, ...), custom_call_target="tpu_custom_call" | custom-call | tf_op jit(solution)/shard_map/pallas_call | solution.py:577
  59.4 2.3 %fusion.1 = f32[4,8,2304]{2,1,0:T(8,128)} fusion(f32[4,8,2304]{2,1,0:T(8,128)} %shard_map.136), kind=kLoop, calls=%fused_computation.2 | loop fusion | flops 4718592 | bytes 589824 | tf_op jit(solution)/shard_map/mul | solution.py:590

commit v5 on v4

--- a/solution.py
+++ b/solution.py
@@ -587,7 +587,7 @@
         state_field, conv_first, conv_second,
         jnp.transpose(spec_real[0], (1, 0, 2)), jnp.transpose(spec_imag[0], (1, 0, 2)), *constants
     )
-    return jax.nn.gelu(before, approximate=False)
+    return gelu(before)
 
 
 def solution(mesh):

time: 61.9 us -> 61.3 us (level)
  no operation moved by 1% of the time
where the time goes in v5:
time: 61.3 us; the launch traced here: 61.2 us
  Pallas kernels  59.4 us (97%)
  other arithmetic  1.73 us (3%)
    pallas_call x1, Pallas kernels, on_device(): pl.pallas_call(kernel, out_shape=jax.ShapeDtypeStruct((NX, NY, C * Z), F3...  59.4 us
    mul x1, other arithmetic, gelu(): return 0.5 * value * (1.0 + lax.erf(value * 0.7071067811865476))  1.73 us

profile of v5, /device:TPU:1, one launch (start us, length us, event | category | flops | bytes accessed | tf_op | source)
XLA Modules:
  0.0 61.2 jit_solution(18160361292462615781)
XLA Ops:
  0.0 59.4 %shard_map.136 = f32[4,8,2304]{2,1,0:T(8,128)} custom-call(f32[4,8,2304]{2,1,0:T(8,128)} %state_hbm.1, f32[3,3,36,108]{3,2,1,0:T(8,128)} %wf_hbm.1, f32[3,3,36,108]{3,2,1,0:T(8,128)} %ws_hbm.1, f32[36,2,432]{2,1,0:T(2,128)} %bitcast.6, f32[36,2,432]{2,1,0:T(2,128)} %bitcast.7, bf16[2,704,256]{2,1,0:T(8,128)(2,1)} %constant.24.clone.fz_hbm, ...), custom_call_target="tpu_custom_call" | custom-call | tf_op jit(solution)/shard_map/pallas_call | solution.py:577
  59.4 1.7 %add_multiply_fusion = f32[4,8,2304]{2,1,0:T(8,128)} fusion(f32[4,8,2304]{2,1,0:T(8,128)} %shard_map.136), kind=kLoop, calls=%fused_computation | loop fusion | flops 294912 | bytes 589824 | tf_op jit(solution)/shard_map/mul | solution.py:106
